TPU v7x, 32 devices: a whole 2x2x4 slice. The times are simulated.
32 devices in a mesh: groups: 2 (over x), tensor: 4 (over y, core), dp: 4 (over z).
Axes of the slice: x: 2, y: 2, z: 4, core: 2. Of those that a mesh axis runs over, the one named last changes fastest.
Arguments:
- hidden_states: bfloat16 [128, 2, 8192], P(('groups', 'tensor', 'dp')), parts along dimension 0, may hold values from -40 to 40
- norm_gain: bfloat16 [8192], replicated, may hold values from 0.099609375 to 1.8984375
- q_blocks: bfloat16 [64, 32, 128, 128], P('tensor'), may hold values from -0.09375 to 0.09375
- q_rows: int32 [64, 32], P('tensor'), may hold values from 0 to 63, as said below
- kv_blocks: bfloat16 [256, 128, 128], P('tensor'), may hold values from -0.09375 to 0.09375
- kv_rows: int32 [256], P('tensor'), may hold values from 0 to 63, as said below
- o_blocks: bfloat16 [64, 32, 128, 128], P('tensor'), may hold values from -0.75 to 0.75
- o_cols: int32 [64, 32], P('tensor'), may hold values from 0 to 63, as said below
- key_cache: bfloat16 [128, 1024, 512], P(('groups', 'tensor', 'dp')), parts along dimension 0, may hold values from -150 to 150
- value_cache: bfloat16 [128, 1024, 512], P(('groups', 'tensor', 'dp')), parts along dimension 0, may hold values from -4 to 4
- lengths: int32 [128], P(('groups', 'tensor', 'dp')), parts along dimension 0, may hold values from 1 to 1024, as said below
Outputs:
- attn_out: bfloat16 [128, 2, 8192], P(('groups', 'tensor', 'dp')), parts along dimension 0
- new_kv: bfloat16 [128, 2, 1024], P(('groups', 'tensor', 'dp')), parts along dimension 0
There are 2 independent parts, one for each index of `groups`. A program takes and returns all parts, laid end to end along the dimension named above; an argument that names none is the same for every part. Nothing has to cross between parts.
Inputs may be any that keep to these rules, and one draw needn't show every extreme that they name: `q_rows`: each row lists 32 different feature blocks in ascending order. `kv_rows`: each aligned run of 32 entries lists 32 different feature blocks in ascending order. `o_cols`: each row lists 32 different column blocks in ascending order. `lengths`: some row has exactly 1024 cached positions and some row exactly 1.
All inputs are finite; a program needn't handle non-finite values.
Results may differ from a plain program's by a relative error of at most 0.007.
The roundings to bfloat16 on the way count: a program that leaves them out, or rounds other values in their place, can miss the bound.
Values may be sent and summed in bfloat16 or wider, within the bound.
A program may use at most 128 MiB of HBM per device.

v0:
```python
import jax
import jax.numpy as jnp
from jax import lax
from jax.sharding import PartitionSpec as P

D = 8192
BLK = 128
QH = 64
KVH = 4
HD = 128
NEW = 2
DB = 64
KEEP = 32
KVCB = 8


def normalize(states, gain):
    widened = states.astype(jnp.float32)
    inv_rms = lax.rsqrt(jnp.mean(widened * widened, axis=-1, keepdims=True) + 1e-05)
    return (widened * inv_rms * gain.astype(jnp.float32)).astype(jnp.bfloat16)


def rotate(vectors, positions):
    half_width = vectors.shape[-1] // 2
    frequency = 500000.0 ** (-jnp.arange(half_width, dtype=jnp.float32) / half_width)
    angles = positions[..., None] * frequency
    cosine = jnp.cos(angles)
    sine_part = jnp.sin(angles)
    lower_half = vectors[..., :half_width]
    upper_half = vectors[..., half_width:]
    return jnp.concatenate(
        [
            lower_half * cosine - upper_half * sine_part,
            upper_half * cosine + lower_half * sine_part,
        ],
        axis=-1,
    )


def attend(queries, fresh_kv, key_cache, value_cache, lengths):
    own_rows = queries.shape[0]
    cache_len = key_cache.shape[1]
    group_size = QH // KVH
    scale = HD ** (-0.5)
    head_match = (
        jnp.arange(KVH, dtype=jnp.int32)[:, None] == jnp.arange(KVH, dtype=jnp.int32)[None, :]
    )
    head_match = head_match[:, None, :, None]
    spread = queries.reshape(own_rows, NEW, KVH, group_size, 1, HD) * head_match.astype(
        jnp.bfloat16
    )
    spread = spread.reshape(own_rows, NEW, QH, KVH * HD)
    fresh_keys = fresh_kv[..., : KVH * HD]
    fresh_values = fresh_kv[..., KVH * HD :]
    cached = (
        jnp.einsum("rjhe,rpe->rjhp", spread, key_cache, preferred_element_type=jnp.float32) * scale
    )
    recent = (
        jnp.einsum("rjhe,rie->rjhi", spread, fresh_keys, preferred_element_type=jnp.float32) * scale
    )
    is_valid = (jnp.arange(cache_len, dtype=jnp.int32)[None, :] < lengths[:, None])[
        :, None, None, :
    ]
    steps_new = jnp.arange(NEW, dtype=jnp.int32)
    causal = (steps_new[None, :] <= steps_new[:, None])[None, :, None, :]
    row_max = jnp.maximum(
        jnp.max(jnp.where(is_valid, cached, -1e30), axis=-1),
        jnp.max(jnp.where(causal, recent, -1e30), axis=-1),
    )
    cache_weights = jnp.where(is_valid, jnp.exp(cached - row_max[..., None]), 0.0).astype(
        jnp.bfloat16
    )
    fresh_weights = jnp.where(causal, jnp.exp(recent - row_max[..., None]), 0.0).astype(
        jnp.bfloat16
    )
    denominator = jnp.sum(cache_weights, axis=-1, dtype=jnp.float32) + jnp.sum(
        fresh_weights, axis=-1, dtype=jnp.float32
    )
    numerator = jnp.einsum(
        "rjhp,rpe->rjhe", cache_weights, value_cache, preferred_element_type=jnp.float32
    )
    numerator = numerator + jnp.einsum(
        "rjhi,rie->rjhe", fresh_weights, fresh_values, preferred_element_type=jnp.float32
    )
    numerator = numerator.reshape(own_rows, NEW, KVH, group_size, KVH, HD) * head_match.astype(
        jnp.float32
    )
    numerator = jnp.sum(numerator, axis=4).reshape(own_rows, NEW, QH, HD)
    return (numerator / denominator[..., None]).reshape(own_rows, NEW, QH * HD).astype(jnp.bfloat16)


def on_device(
    hidden_states,
    norm_gain,
    q_blocks,
    q_rows,
    kv_blocks,
    kv_rows,
    o_blocks,
    o_cols,
    key_cache,
    value_cache,
    lengths,
):
    own_rows = hidden_states.shape[0]
    tp_size = lax.axis_size("tensor")
    tp_index = lax.axis_index("tensor")
    group_rows = own_rows * tp_size
    tokens = group_rows * NEW
    heads_here = QH // tp_size
    gathered = normalize(lax.all_gather(hidden_states, "tensor", axis=0, tiled=True), norm_gain)
    blocks_in = gathered.reshape(tokens, DB, BLK)
    picked = jnp.take(blocks_in, q_rows, axis=1)
    queries_raw = jnp.einsum("tckb,ckbe->tce", picked, q_blocks, preferred_element_type=jnp.float32)
    queries_raw = queries_raw.astype(jnp.bfloat16).reshape(group_rows, NEW, heads_here * HD)
    entries = kv_blocks.shape[0]
    kv_in = jnp.take(blocks_in, kv_rows, axis=1)
    contrib = jnp.einsum("teb,ebc->tec", kv_in, kv_blocks, preferred_element_type=jnp.float32)
    columns = (tp_index * entries + jnp.arange(entries, dtype=jnp.int32)) // KEEP
    onehot = (columns[:, None] == jnp.arange(KVCB, dtype=jnp.int32)[None, :]).astype(jnp.float32)
    kv_part = jnp.einsum("tec,ek->tkc", contrib, onehot, precision=lax.Precision.HIGHEST).reshape(
        group_rows, NEW, KVCB * BLK
    )
    queries_mine = lax.all_to_all(queries_raw, "tensor", split_axis=0, concat_axis=2, tiled=True)
    kv_sum = lax.psum_scatter(kv_part, "tensor", scatter_dimension=0, tiled=True)
    positions = (lengths[:, None] + jnp.arange(NEW, dtype=jnp.int32)[None, :]).astype(jnp.float32)
    queries = rotate(
        queries_mine.astype(jnp.float32).reshape(own_rows, NEW, QH, HD), positions[..., None]
    ).astype(jnp.bfloat16)
    keys_new = rotate(kv_sum[..., : KVH * HD].reshape(own_rows, NEW, KVH, HD), positions[..., None])
    new_kv = jnp.concatenate(
        [keys_new.reshape(own_rows, NEW, KVH * HD), kv_sum[..., KVH * HD :]], axis=-1
    ).astype(jnp.bfloat16)
    attended = attend(queries, new_kv, key_cache, value_cache, lengths)
    returned = lax.all_to_all(attended, "tensor", split_axis=2, concat_axis=0, tiled=True)
    row_blocks_here = heads_here * HD // BLK
    o_in = returned.reshape(tokens, row_blocks_here, BLK)
    out_terms = jnp.einsum("tib,ikbc->tikc", o_in, o_blocks, preferred_element_type=jnp.float32)
    place_onehot = (
        o_cols.reshape(row_blocks_here * KEEP)[:, None] == jnp.arange(DB, dtype=jnp.int32)[None, :]
    ).astype(jnp.float32)
    partial_value = jnp.einsum(
        "tec,en->tnc",
        out_terms.reshape(tokens, row_blocks_here * KEEP, BLK),
        place_onehot,
        precision=lax.Precision.HIGHEST,
    )
    partial_value = partial_value.reshape(group_rows, NEW, D)
    reduced = lax.psum_scatter(partial_value, "tensor", scatter_dimension=0, tiled=True).astype(
        jnp.bfloat16
    )
    return (reduced, new_kv)


def solution(mesh):
    return jax.shard_map(
        on_device,
        mesh=mesh,
        in_specs=(
            P(("groups", "tensor", "dp"), None, None),
            P(),
            P("tensor", None, None, None),
            P("tensor", None),
            P("tensor", None, None),
            P("tensor"),
            P("tensor", None, None, None),
            P("tensor", None),
            P(("groups", "tensor", "dp"), None, None),
            P(("groups", "tensor", "dp"), None, None),
            P(("groups", "tensor", "dp")),
        ),
        out_specs=(
            P(("groups", "tensor", "dp"), None, None),
            P(("groups", "tensor", "dp"), None, None),
        ),
        check_vma=False,
    )
```

profile of v0, /device:TPU:0, one launch (start us, length us, event | category | flops | bytes accessed | tf_op | source)
XLA Modules:
  0.0 169.0 jit_solution(17563405291816128651)
XLA Ops:
  7.2 0.0 copy-start
  7.2 0.0 all-reduce.5.cloned.1.call-start
  7.2 0.8 compare_select_fusion.1
  8.0 0.7 compare_and_fusion.1
  8.7 8.8 %all_gather.3 = bf16[16,2,8192]{2,1,0:T(2,128)(2,1)S(1)} all-gather(bf16[4,2,8192]{2,1,0:T(2,128)(2,1)} %param.11), channel_id=1, replica_groups=mesh['groups'=2,'tensor'=4,'dp'=4] {'tensor'}, dimensions={0}, use_global_device_ids=true | all-gather | bytes 655360 | tf_op jit(solution)/shard_map/all_gather | solution.py:111
  17.5 0.6 fusion.27
  18.2 0.7 convert_element_type.80
  18.9 0.7 fusion.29
  19.6 0.0 copy-start.2
  19.6 0.4 reshape.207
  20.0 0.3 copy.35
  20.4 0.7 gather_fusion.1
  21.0 0.7 convolution_bitcast_fusion
  21.8 1.0 convolution_bitcast_fusion.1
  22.8 0.7 reshape.209
  23.5 0.0 all-reduce.5.cloned.1.call-update
  23.6 0.1 reshape.221
  23.7 3.4 %gather_fusion = bf16[512,32,128]{2,1,0:T(8,128)(2,1)} fusion(bf16[32,64,128]{2,0,1:T(8,128)(2,1)S(1)} %copy.35, s32[1024]{0:T(1024)S(1)} %pad_clamp_fusion.1), kind=kCustom, calls=%fused_computation | custom fusion | bytes 8390656 | tf_op jit(solution)/shard_map/jit(_take)/gather | solution.py:113
  27.1 8.7 %fusion.24 = bf16[32,16,128]{2,0,1:T(8,128)(2,1)S(1)} fusion(bf16[16,32,128,128]{3,2,1,0:T(8,128)(2,1)} %param.13, bf16[16,32,32,128]{3,2,1,0:T(8,128)(2,1)} %bitcast.93, pred[16,32]{1,0:T(8,128)(4,1)S(1)} %compare_and_fusion), kind=kOutput, calls=%fused_computation.26 | convolution fusion | flops 539033600 | bytes 21103104 | tf_op jit(solution)/shard_map/tckb,ckbe->tce/dot_general | solution.py:114
  35.8 0.1 copy.36
  35.9 0.7 reshape.208
  36.5 3.5 %all-to-all-start = ((bf16[16,2,2048]{2,1,0:T(2,128)(2,1)}), bf16[16,2,2048]{2,1,0:T(2,128)(2,1)S(1)}, u32[]{:S(2)}, u32[]{:S(2)}) async-start(bf16[16,2,2048]{2,1,0:T(2,128)(2,1)} %reshape.208), calls=%async_computation | async-start | bytes 262144 | tf_op jit(solution)/shard_map/all_to_all | solution.py:124
  40.1 0.1 add_convert_fusion.2
  40.2 0.1 iota_compare_fusion.1
  40.3 0.1 mul.162
  40.4 0.1 eq.56
  40.5 0.6 dynamic-slice
  41.7 0.1 multiply_cosine_fusion
  41.9 14.1 %all-reduce.5.cloned.1.call-done = f32[16,2,1024]{2,1,0:T(2,128)} async-done(((f32[16,2,1024]{2,1,0:T(2,128)}), f32[16,2,1024]{2,1,0:T(2,128)}) %all-reduce.5.cloned.1.call-update) | async-done | bytes 131088
  56.0 0.7 constant_dynamic-slice_fusion
  56.7 0.1 subtract_convert_fusion.1
  56.8 0.1 pad_maximum_fusion.2
  56.9 0.8 dynamic-slice_convert_fusion.1
  57.7 0.1 convert_bitcast_fusion
  57.9 0.2 copy.37
  58.0 0.1 reshape.217
  58.2 0.1 subtract_convert_fusion
  58.3 0.1 pad_maximum_fusion
  58.5 0.2 mul.160
  58.7 0.2 mul.161
  58.9 0.3 select_reduce_fusion.1
  59.3 3.8 %select_reduce_fusion = (f32[4,2,64]{2,1,0:T(2,128)S(1)}, f32[4,2,64,1024]{3,2,1,0:T(8,128)S(1)}) fusion(pred[4,1024]{1,0:T(4,128)(4,1)S(1)} %iota_compare_fusion.1, bf16[4,1024,512]{2,1,0:T(8,128)(2,1)} %param.19, bf16[4,2,64,512]{3,2,1,0:T(8,128)(2,1)S(1)} %mul.161, bf16[64,512]{1,0:T(8,128)(2,1)S(1)} %bitcast.98), kind=kOutput, calls=%fused_computation.17 | convolution fusion | flops 538705408 | bytes 6887424 | tf_op jit(solution)/shard_map/rjhe,rpe->rjhp/dot_general | solution.py:56
  63.0 0.1 convert_reduce_fusion.1
  63.1 0.6 convert_reduce_fusion
  63.7 0.1 copy.40
  63.9 0.3 fusion.44
  64.2 3.1 %fusion.12 = f32[4,2,64,512]{3,2,1,0:T(8,128)S(1)} fusion(f32[4,2,64,512]{3,2,1,0:T(8,128)S(1)} %fusion.44, bf16[4,1024,512]{2,1,0:T(8,128)(2,1)} %param.20, f32[4,2,64,1024]{3,2,1,0:T(8,128)S(1)} %get-tuple-element.11, f32[4,2,64]{2,1,0:T(2,128)S(1)} %max.7, pred[4,1024]{1,0:T(4,128)(4,1)S(1)} %iota_compare_fusion.1), kind=kOutput, calls=%fused_computation.19 | convolution fusion | flops 539230208 | bytes 8394752 | tf_op jit(solution)/shard_map/rjhp,rpe->rjhe/dot_general | solution.py:79
  67.3 0.4 reshape.212
  67.7 0.7 multiply_reduce_fusion
  68.5 5.9 %copy.52 = f32[4,2,4,16,128]{0,1,4,3,2:T(2,128)} copy(f32[4,2,4,16,128]{4,3,2,1,0:T(8,128)S(1)} %multiply_reduce_fusion) | data formatting | bytes 524288 | tf_op jit(solution)/shard_map/reshape | solution.py:88
  74.3 6.9 %fusion.2 = bf16[4,2,8192]{0,1,2:T(2,128)(2,1)} fusion(f32[4,2,4,16,128]{0,1,4,3,2:T(2,128)} %copy.52, f32[4,2,64]{0,1,2:T(2,128)S(1)} %copy.40), kind=kLoop, calls=%fused_computation.5 | loop fusion | flops 131072 | bytes 395264 | tf_op jit(solution)/shard_map/convert_element_type | solution.py:89
  81.3 9.3 %reshape.249 = bf16[4,2,8192]{2,1,0:T(2,128)(2,1)} reshape(bf16[8192,2,4]{2,1,0:T(2,128)(2,1)} %bitcast.94) | data formatting | bytes 262144
  90.6 3.5 %all-to-all-start.1 = ((bf16[4,2,8192]{2,1,0:T(2,128)(2,1)}), bf16[4,2,8192]{2,1,0:T(2,128)(2,1)S(1)}, u32[]{:S(2)}, u32[]{:S(2)}) async-start(bf16[4,2,8192]{2,1,0:T(2,128)(2,1)} %reshape.249), calls=%async_computation.1 | async-start | bytes 262144 | tf_op jit(solution)/shard_map/all_to_all | solution.py:135
  94.2 0.6 pad_maximum_fusion.1
  94.8 3.8 %all-to-all-done.1 = bf16[4,2,8192]{2,1,0:T(2,128)(2,1)S(1)} async-done(((bf16[4,2,8192]{2,1,0:T(2,128)(2,1)}), bf16[4,2,8192]{2,1,0:T(2,128)(2,1)S(1)}, u32[]{:S(2)}, u32[]{:S(2)}) %all-to-all-start.1) | async-done | bytes 131104 | tf_op jit(solution)/shard_map/all_to_all | solution.py:135
  98.5 10.0 %reshape.250 = bf16[8192,2,4]{2,1,0:T(2,128)(2,1)} reshape(bf16[4,2,8192]{2,1,0:T(2,128)(2,1)S(1)} %all-to-all-done.1) | data formatting | bytes 262144
  108.5 9.7 %copy.53 = bf16[4,2,4,2048]{3,2,1,0:T(4,128)(2,1)S(1)} copy(bf16[4,2,4,2048]{0,1,3,2:T(2,128)(2,1)} %bitcast.95) | data formatting | bytes 262144 | tf_op jit(solution)/shard_map/all_to_all | solution.py:135
  118.3 0.1 copy.43
  118.4 0.1 reshape.214
  118.5 7.0 %fusion.39 = f32[16,32,32,128]{3,1,2,0:T(8,128)S(1)} fusion(bf16[16,32,128,128]{3,2,1,0:T(8,128)(2,1)} %param.17, bf16[32,16,128,1]{2,1,0,3:T(8,128)(2,1)S(1)} %bitcast.96), kind=kOutput, calls=%fused_computation.46 | convolution fusion | flops 536870912 | bytes 25296896 | tf_op jit(solution)/shard_map/tib,ikbc->tikc/dot_general | solution.py:138
  125.6 8.1 %fusion.15 = f32[32,64,128]{2,1,0:T(8,128)S(1)} fusion(f32[32,512,128]{2,0,1:T(8,128)S(1)} %bitcast.92, s32[512]{0:T(512)S(1)} %eq.56), kind=kOutput, calls=%fused_computation.20 | convolution fusion | flops 1610645504 | bytes 9439232 | tf_op jit(solution)/shard_map/tec,en->tnc/dot_general | solution.py:142
  133.6 1.6 reshape.216
  135.2 26.2 %all-reduce.6 = bf16[16,2,8192]{2,1,0:T(2,128)(2,1)S(1)} all-reduce(f32[16,2,8192]{2,1,0:T(2,128)} %reshape.216), channel_id=3, replica_groups=mesh['groups'=2,'tensor'=4,'dp'=4] {'tensor'}, use_global_device_ids=true, to_apply=%region_7.8.clone | all-reduce | flops 262144 | bytes 1572864
  161.4 0.8 dynamic-slice_convert_fusion
  (27 shorter events, 0.2 us)
Async XLA Ops:
  7.2 13.9 %copy-start = (bf16[64,128,128]{2,1,0:T(8,128)(2,1)S(1)}, bf16[64,128,128]{2,1,0:T(8,128)(2,1)}, u32[]{:S(2)}) copy-start(bf16[64,128,128]{2,1,0:T(8,128)(2,1)} %param.15) | copy-start | bytes 6291460
  7.2 48.8 %all-reduce.5.cloned.1.call-start = ((), (), s32[]{:S(2)}) async-start(), calls=%async_computation.2 | async-start | bytes 262144
  19.6 4.0 %copy-start.2 = (s32[16,32]{1,0:T(8,128)S(1)}, s32[16,32]{1,0:T(8,128)}, u32[]{:S(2)}) copy-start(s32[16,32]{1,0:T(8,128)} %param.14) | copy-start | bytes 6148
  27.1 13.0 %copy-start.4 = (s32[4]{0:T(128)S(1)}, s32[4]{0:T(128)}, u32[]{:S(2)}) copy-start(s32[4]{0:T(128)} %param.21) | copy-start | bytes 52
  27.1 13.3 %copy-start.3 = (s32[16,32]{1,0:T(8,128)S(1)}, s32[16,32]{1,0:T(8,128)}, u32[]{:S(2)}) copy-start(s32[16,32]{1,0:T(8,128)} %param.18) | copy-start | bytes 6148
  27.1 13.4 %copy-start.5 = (u32[32]{0:T(128)S(1)}, u32[32]{0:T(128)}, u32[]{:S(2)}) copy-start(u32[32]{0:T(128)} %constant.74) | copy-start | bytes 388
  36.5 21.2 %all-to-all-start = ((bf16[16,2,2048]{2,1,0:T(2,128)(2,1)}), bf16[16,2,2048]{2,1,0:T(2,128)(2,1)S(1)}, u32[]{:S(2)}, u32[]{:S(2)}) async-start(bf16[16,2,2048]{2,1,0:T(2,128)(2,1)} %reshape.208), calls=%async_computation | async-start | bytes 262144 | tf_op jit(solution)/shard_map/all_to_all | solution.py:124
  90.6 7.9 %all-to-all-start.1 = ((bf16[4,2,8192]{2,1,0:T(2,128)(2,1)}), bf16[4,2,8192]{2,1,0:T(2,128)(2,1)S(1)}, u32[]{:S(2)}, u32[]{:S(2)}) async-start(bf16[4,2,8192]{2,1,0:T(2,128)(2,1)} %reshape.249), calls=%async_computation.1 | async-start | bytes 262144 | tf_op jit(solution)/shard_map/all_to_all | solution.py:135
  125.5 36.6 %copy-start.1 = (bf16[64,128,128]{2,1,0:T(8,128)(2,1)S(1)}, bf16[64,128,128]{2,1,0:T(8,128)(2,1)}, u32[]{:S(2)}) copy-start(bf16[64,128,128]{2,1,0:T(8,128)(2,1)} %param.15) | copy-start | bytes 6291460
Sparse Core Ops, SparseCore 0:
  23.7 32.2 all-reduce.4
where the time goes:
time: 170 us; the launch traced here: 169 us
  local copies, waits for them, and re-layouts  47.5 us (28%)
  blocking collectives  35 us (21%)
  matrix products  33.1 us (19%)
  waiting for transfers between devices  17.9 us (11%)
  between operations  15 us (9%)
  other arithmetic  13.4 us (8%)
  starting transfers between devices  7.09 us (4%)
    unnamed x1, blocking collectives  26.2 us
    unnamed x16, local copies, waits for them, and re-layouts  20 us
    unnamed x2, waiting for transfers between devices  14.1 us
    all_to_all x2, local copies, waits for them, and re-layouts, on_device(): lax.all_to_all(attended, 'tensor', split_axis=2, concat_axis=0, tiled=True)  9.86 us
    all_gather x1, blocking collectives, on_device(): lax.all_gather(hidden_states, 'tensor', axis=0, tiled=True)  8.84 us
    dot_general x1, matrix products, on_device(): jnp.einsum('tckb,ckbe->tce', picked, q_blocks, preferred_element_type=jnp...  8.69 us
    dot_general x1, matrix products, on_device(): jnp.einsum('tec,en->tnc', out_terms.reshape(tokens, row_blocks_here * KEE...  8.06 us
    dot_general x1, matrix products, on_device(): jnp.einsum('tib,ikbc->tikc', o_in, o_blocks, preferred_element_type=jnp.f...  7.02 us
  transfers between devices with their start and end apart: 3, of which 2 were waited for; matrix products, arithmetic and copies ran while one was open for 10% of the time, Pallas kernels for 0%

commit v1 on v0

v1 whole, which is shorter than its diff:
```python
import functools

import jax
import jax.numpy as jnp
from jax import lax
from jax.experimental import pallas as pl
from jax.experimental.pallas import tpu as pltpu
from jax.sharding import PartitionSpec as P

D = 8192
BLK = 128
QH = 64
KVH = 4
HD = 128
NEW = 2
DB = 64
KEEP = 32
KVCB = 8
ROW_DEV = 4
OWN = ROW_DEV * NEW
GROUP = QH // KVH
PAD = 128
CHUNKS = 8
MESH = pl.DeviceIdType.MESH
F32 = jnp.float32
BF16 = jnp.bfloat16


def kernel(
    tp,
    hh,
    entries,
    cache_len,
    hidden,
    gain,
    cosine,
    sine,
    q_rows,
    kv_rows,
    place,
    lengths,
    q_hbm,
    kv_hbm,
    o_hbm,
    k_hbm,
    v_hbm,
    out,
    new_kv,
    wq,
    wkv,
    wo,
    kbuf,
    vbuf,
    nf,
    xg,
    qs,
    qr,
    qf,
    ks,
    kr,
    af,
    asend,
    ar,
    xo,
    pbuf,
    rbuf,
    sbuf,
    fbuf,
    q_sem,
    kv_sem,
    o_sem,
    c_sem,
    x1_sem,
    x2_sem,
    x3_sem,
    qa_sem,
    ka_sem,
    aa_sem,
    s1_sem,
    s2_sem,
):
    ny = tp // 2
    me = lax.axis_index("tensor")
    my = me // 2
    mc = lax.rem(me, 2)
    other = my * 2 + (1 - mc)

    q_copies = [pltpu.make_async_copy(q_hbm.at[c], wq.at[c], q_sem.at[c]) for c in range(hh)]
    kv_copy = pltpu.make_async_copy(kv_hbm, wkv, kv_sem)
    k_copies = [
        pltpu.make_async_copy(k_hbm.at[r], kbuf.at[r, pl.ds(0, cache_len)], c_sem.at[0, r])
        for r in range(ROW_DEV)
    ]
    v_copies = [
        pltpu.make_async_copy(v_hbm.at[r], vbuf.at[r, pl.ds(0, cache_len)], c_sem.at[1, r])
        for r in range(ROW_DEV)
    ]
    o_copies = [
        pltpu.make_async_copy(o_hbm.at[i], wo.at[pl.ds(i * KEEP, KEEP)], o_sem.at[i])
        for i in range(hh)
    ]
    kv_copy.start()
    for copy in q_copies + k_copies + v_copies + o_copies:
        copy.start()

    def remote(src, dst, sems, slot, target):
        return pltpu.make_async_remote_copy(
            src_ref=src,
            dst_ref=dst,
            send_sem=sems.at[(0,) + slot],
            recv_sem=sems.at[(1,) + slot],
            device_id={"tensor": target},
            device_id_type=MESH,
        )

    barrier = pltpu.get_barrier_semaphore()
    for step in range(1, tp):
        pl.semaphore_signal(
            barrier, inc=1, device_id={"tensor": lax.rem(me + step, tp)}, device_id_type=MESH
        )

    wide = hidden[...].astype(F32)
    inv_rms = lax.rsqrt(jnp.mean(wide * wide, axis=-1, keepdims=True) + 1e-05)
    normed = (wide * inv_rms * gain[...].astype(F32)).astype(BF16).astype(F32)
    for b in range(DB):
        nf[mc, b] = normed[:, b * BLK : (b + 1) * BLK]
    wo[hh * KEEP] = jnp.zeros((BLK, BLK), BF16)

    pl.semaphore_wait(barrier, tp - 1)

    x1 = remote(nf.at[mc], nf.at[mc], x1_sem, (0,), other)
    x1.start()
    x1_in = remote(nf.at[1 - mc], nf.at[1 - mc], x1_sem, (0,), other)
    x1_in.wait_recv()
    xg[my] = jnp.concatenate([nf[0], nf[1]], axis=1).astype(BF16)

    half = DB // 2
    mine = pl.ds(mc * half, half)
    theirs = pl.ds((1 - mc) * half, half)
    x2 = []
    for step in range(1, ny):
        to = lax.rem(my + step, ny)
        copy = remote(xg.at[my, mine], xg.at[my, mine], x2_sem, (step,), to * 2 + mc)
        copy.start()
        x2.append(copy)
    x3 = []
    for step in range(1, ny):
        source = lax.rem(my + ny - step, ny)
        piece = xg.at[source, mine]
        remote(piece, piece, x2_sem, (step,), other).wait_recv()
        copy = remote(piece, piece, x3_sem, (step,), other)
        copy.start()
        x3.append(copy)
    for step in range(1, ny):
        source = lax.rem(my + ny - step, ny)
        piece = xg.at[source, theirs]
        remote(piece, piece, x3_sem, (step,), other).wait_recv()

    def picked(rows):
        blocks = [jnp.concatenate([xg[y, row] for y in range(ny)], axis=0) for row in rows]
        return jnp.concatenate(blocks, axis=1)

    kv_copy.wait()
    cols = max(1, entries // KEEP)
    per = entries // cols
    for col in range(cols):
        x = picked([kv_rows[col * per + e] for e in range(per)])
        w = wkv[pl.ds(col * per, per)].reshape(per * BLK, BLK)
        part = jnp.dot(x, w, preferred_element_type=F32)
        for d in range(tp):
            ks[d, pl.ds(col * OWN, OWN)] = part[d * OWN : (d + 1) * OWN]
    sends = []
    for step in range(1, tp):
        to = lax.rem(me + step, tp)
        copy = remote(ks.at[to], kr.at[me], ka_sem, (step,), to)
        copy.start()
        sends.append(copy)
    kr[me] = ks[me]

    for copy in q_copies:
        copy.wait()

    def query_pair(pair, carry):
        parts = []
        for s in range(2):
            c = pair * 2 + s
            x = picked([q_rows[c * KEEP + k] for k in range(KEEP)])
            w = wq[c].reshape(KEEP * BLK, BLK)
            parts.append(jnp.dot(x, w, preferred_element_type=F32))
        for d in range(tp):
            both = jnp.concatenate([p[d * OWN : (d + 1) * OWN] for p in parts], axis=0)
            qs[d, pl.ds(pl.multiple_of(pair * 16, 16), 16)] = both.astype(BF16)
        return carry

    lax.fori_loop(0, hh // 2, query_pair, 0)
    slab = hh * OWN
    for step in range(1, tp):
        to = lax.rem(me + step, tp)
        copy = remote(qs.at[to], qr.at[me], qa_sem, (step,), to)
        copy.start()
        sends.append(copy)
    qr[me] = qs[me]

    cos_own = cosine[...]
    sin_own = sine[...]
    for step in range(1, tp):
        source = lax.rem(me + tp - step, tp)
        remote(ks.at[source], kr.at[source], ka_sem, (step,), source).wait_recv()
    share = max(1, KEEP // entries)
    fresh = []
    for col in range(KVCB):
        if share == 1:
            total = kr[col // cols, pl.ds((col % cols) * OWN, OWN)]
        else:
            total = kr[col * share]
            for extra in range(1, share):
                total = total + kr[col * share + extra]
        if col < KVH:
            total = total * cos_own + pltpu.roll(total, HD // 2, 1) * sin_own
        fresh.append(total)
    fresh = jnp.concatenate(fresh, axis=1).astype(BF16)
    new_kv[...] = fresh
    tail = jnp.concatenate(
        [fresh.astype(F32), jnp.zeros((PAD - OWN, 2 * KVH * HD), F32)], axis=0
    ).astype(BF16)
    for r in range(ROW_DEV):
        kbuf[r, pl.ds(cache_len, PAD)] = tail[:, : KVH * HD]
        vbuf[r, pl.ds(cache_len, PAD)] = tail[:, KVH * HD :]

    for step in range(1, tp):
        source = lax.rem(me + tp - step, tp)
        remote(qs.at[source], qr.at[source], qa_sem, (step,), source).wait_recv()
    for s in range(tp):
        raw = qr[s].astype(F32)
        swapped = pltpu.roll(raw, HD // 2, 1)
        turned = raw.reshape(hh, OWN, HD) * cos_own[None] + swapped.reshape(hh, OWN, HD) * sin_own[None]
        qf[pl.ds(s * slab, slab)] = turned.reshape(slab, HD)
    for copy in k_copies + v_copies:
        copy.wait()

    width = cache_len + PAD
    scale = HD ** (-0.5)
    spot = lax.broadcasted_iota(jnp.int32, (NEW * GROUP, width), 1)
    token = lax.broadcasted_iota(jnp.int32, (NEW * GROUP, width), 0) // GROUP

    def attend_row(r, carry):
        first = cache_len + NEW * r
        valid = (spot < lengths[r]) | ((spot >= first) & (spot <= first + token))
        for g in range(KVH):
            q = jnp.concatenate(
                [qf[pl.ds(g * GROUP * OWN + NEW * r + j, GROUP, stride=OWN)] for j in range(NEW)],
                axis=0,
            ).astype(BF16)
            keys = kbuf[r, :, g * HD : (g + 1) * HD]
            scores = lax.dot_general(
                q, keys, (((1,), (1,)), ((), ())), preferred_element_type=F32
            )
            scores = jnp.where(valid, scores * scale, -1e30)
            top = jnp.max(scores, axis=-1, keepdims=True)
            weights = jnp.where(valid, jnp.exp(scores - top), 0.0).astype(BF16)
            below = jnp.sum(weights.astype(F32), axis=-1, keepdims=True)
            values = vbuf[r, :, g * HD : (g + 1) * HD]
            above = jnp.dot(weights, values, preferred_element_type=F32)
            result = above / below
            for j in range(NEW):
                af[pl.ds(g * GROUP * OWN + NEW * r + j, GROUP, stride=OWN)] = result[
                    j * GROUP : (j + 1) * GROUP
                ]
        return carry

    lax.fori_loop(0, ROW_DEV, attend_row, 0)

    for d in range(tp):
        asend[d] = af[pl.ds(d * slab, slab)].astype(BF16)
    for step in range(1, tp):
        to = lax.rem(me + step, tp)
        copy = remote(asend.at[to], ar.at[me], aa_sem, (step,), to)
        copy.start()
        sends.append(copy)
    ar[me] = asend[me]
    for copy in o_copies:
        copy.wait()
    for step in range(1, tp):
        source = lax.rem(me + tp - step, tp)
        remote(asend.at[source], ar.at[source], aa_sem, (step,), source).wait_recv()

    order = [y * 2 + c for c in range(2) for y in range(ny)]
    heads = [ar[s].astype(F32) for s in order]
    for i in range(hh):
        lhs = jnp.concatenate([h[i * OWN : (i + 1) * OWN] for h in heads], axis=0)
        xo[:, i * BLK : (i + 1) * BLK] = lhs.astype(BF16)

    pairs = DB // CHUNKS // 2
    side = ny * OWN

    def stage1(ch):
        return remote(pbuf.at[ch, 1 - mc], rbuf.at[ch], s1_sem, (ch,), other)

    def stage2(ch, step):
        to = lax.rem(my + step, ny)
        piece = sbuf.at[ch, pl.ds(pl.multiple_of(to * OWN, OWN), OWN)]
        return remote(piece, fbuf.at[ch, my], s2_sem, (ch, step), to * 2 + mc)

    def pass_on(ch):
        stage1(ch).wait_recv()
        sbuf[ch] = pbuf[ch, mc] + rbuf[ch]
        for step in range(1, ny):
            stage2(ch, step).start()

    def project(ch, carry):
        def one_pair(pair, inner):
            n = (ch * pairs + pair) * 2
            total = None
            wide_k = 2 if hh % 2 == 0 else 1
            for i in range(0, hh, wide_k):
                w = jnp.concatenate(
                    [
                        jnp.concatenate(
                            [wo[place[(n + a) * hh + i + b]] for b in range(wide_k)], axis=0
                        )
                        for a in range(2)
                    ],
                    axis=1,
                )
                part = jnp.dot(
                    xo[:, i * BLK : (i + wide_k) * BLK], w, preferred_element_type=F32
                )
                total = part if total is None else total + part
            columns = pl.ds(pl.multiple_of(pair * 2 * BLK, 2 * BLK), 2 * BLK)
            for c in range(2):
                pbuf[ch, c, :, columns] = total[c * side : (c + 1) * side]
            return inner

        lax.fori_loop(0, pairs, one_pair, 0)
        stage1(ch).start()

        @pl.when(ch > 0)
        def _():
            pass_on(ch - 1)

        return carry

    lax.fori_loop(0, CHUNKS, project, 0)
    pass_on(CHUNKS - 1)

    def finish(ch, carry):
        total = sbuf[ch, pl.ds(pl.multiple_of(my * OWN, OWN), OWN)]
        for step in range(1, ny):
            source = lax.rem(my + ny - step, ny)
            remote(
                sbuf.at[ch, pl.ds(0, OWN)], fbuf.at[ch, source], s2_sem, (ch, step), other
            ).wait_recv()
            total = total + fbuf[ch, source]
        wide_chunk = D // CHUNKS
        out[:, pl.ds(pl.multiple_of(ch * wide_chunk, wide_chunk), wide_chunk)] = total.astype(BF16)
        return carry

    lax.fori_loop(0, CHUNKS, finish, 0)

    x1.wait_send()
    for copy in x2 + x3 + sends:
        copy.wait_send()

    def drain(ch, carry):
        stage1(ch).wait_send()
        for step in range(1, ny):
            stage2(ch, step).wait_send()
        return carry

    lax.fori_loop(0, CHUNKS, drain, 0)


def on_device(
    tp,
    hidden_states,
    norm_gain,
    q_blocks,
    q_rows,
    kv_blocks,
    kv_rows,
    o_blocks,
    o_cols,
    key_cache,
    value_cache,
    lengths,
):
    hh = q_blocks.shape[0]
    entries = kv_blocks.shape[0]
    cache_len = key_cache.shape[1]
    ny = tp // 2
    half = HD // 2
    frequency = 500000.0 ** (-jnp.arange(half, dtype=F32) / half)
    positions = (lengths[:, None] + jnp.arange(NEW, dtype=jnp.int32)[None, :]).astype(F32)
    angles = positions.reshape(OWN, 1) * frequency
    cos_half, sin_half = jnp.cos(angles), jnp.sin(angles)
    cosine = jnp.concatenate([cos_half, cos_half], axis=-1)
    sine = jnp.concatenate([-sin_half, sin_half], axis=-1)
    slot = jnp.arange(hh * KEEP, dtype=jnp.int32).reshape(hh, KEEP)
    hit = o_cols[None] == jnp.arange(DB, dtype=jnp.int32)[:, None, None]
    place = jnp.min(jnp.where(hit, slot[None], hh * KEEP), axis=-1).reshape(DB * hh)

    vmem = pl.BlockSpec(memory_space=pltpu.VMEM)
    smem = pl.BlockSpec(memory_space=pltpu.SMEM)
    anywhere = pl.BlockSpec(memory_space=pl.ANY)
    slab = hh * OWN
    cols = max(1, entries // KEEP)
    width = cache_len + PAD
    chunk = D // CHUNKS
    dma = pltpu.SemaphoreType.DMA
    out, new_kv = pl.pallas_call(
        functools.partial(kernel, tp, hh, entries, cache_len),
        out_shape=(
            jax.ShapeDtypeStruct((OWN, D), BF16),
            jax.ShapeDtypeStruct((OWN, 2 * KVH * HD), BF16),
        ),
        in_specs=[vmem] * 4 + [smem] * 4 + [anywhere] * 5,
        out_specs=(vmem, vmem),
        scratch_shapes=[
            pltpu.VMEM((hh, KEEP, BLK, BLK), BF16),
            pltpu.VMEM((entries, BLK, BLK), BF16),
            pltpu.VMEM((hh * KEEP + 1, BLK, BLK), BF16),
            pltpu.VMEM((ROW_DEV, width, KVH * HD), BF16),
            pltpu.VMEM((ROW_DEV, width, KVH * HD), BF16),
            pltpu.VMEM((2, DB, OWN, BLK), F32),
            pltpu.VMEM((ny, DB, 2 * OWN, BLK), BF16),
            pltpu.VMEM((tp, slab, HD), BF16),
            pltpu.VMEM((tp, slab, HD), BF16),
            pltpu.VMEM((tp * slab, HD), F32),
            pltpu.VMEM((tp, cols * OWN, BLK), F32),
            pltpu.VMEM((tp, cols * OWN, BLK), F32),
            pltpu.VMEM((tp * slab, HD), F32),
            pltpu.VMEM((tp, slab, HD), BF16),
            pltpu.VMEM((tp, slab, HD), BF16),
            pltpu.VMEM((tp * OWN, hh * BLK), BF16),
            pltpu.VMEM((CHUNKS, 2, ny * OWN, chunk), F32),
            pltpu.VMEM((CHUNKS, ny * OWN, chunk), F32),
            pltpu.VMEM((CHUNKS, ny * OWN, chunk), F32),
            pltpu.VMEM((CHUNKS, ny, OWN, chunk), F32),
            dma((hh,)),
            dma,
            dma((hh,)),
            dma((2, ROW_DEV)),
            dma((2, 1)),
            dma((2, ny)),
            dma((2, ny)),
            dma((2, tp)),
            dma((2, tp)),
            dma((2, tp)),
            dma((2, CHUNKS)),
            dma((2, CHUNKS, ny)),
        ],
        compiler_params=pltpu.CompilerParams(
            collective_id=0, has_side_effects=True, vmem_limit_bytes=60 * 1024 * 1024
        ),
    )(
        hidden_states.reshape(OWN, D),
        norm_gain.reshape(1, D),
        cosine,
        sine,
        q_rows.reshape(hh * KEEP),
        kv_rows,
        place,
        lengths,
        q_blocks,
        kv_blocks,
        o_blocks,
        key_cache,
        value_cache,
    )
    return out.reshape(ROW_DEV, NEW, D), new_kv.reshape(ROW_DEV, NEW, 2 * KVH * HD)


def solution(mesh):
    rows = P(("groups", "tensor", "dp"), None, None)
    return jax.shard_map(
        functools.partial(on_device, mesh.shape["tensor"]),
        mesh=mesh,
        in_specs=(
            rows,
            P(),
            P("tensor", None, None, None),
            P("tensor", None),
            P("tensor", None, None),
            P("tensor"),
            P("tensor", None, None, None),
            P("tensor", None),
            rows,
            rows,
            P(("groups", "tensor", "dp")),
        ),
        out_specs=(rows, rows),
        check_vma=False,
    )
```

time: 170 us -> 59.3 us (0.35)
  Pallas kernels: 0 us -> 47.6 us
  local copies, waits for them, and re-layouts: 47.5 us -> 8.12 us
  blocking collectives: 35 us -> 0 us
  matrix products: 33.1 us -> 0 us
  waiting for transfers between devices: 17.9 us -> 0 us
  between operations: 15 us -> 0.65 us
  other arithmetic: 13.4 us -> 2.44 us
  starting transfers between devices: 7.09 us -> 0 us
    pallas_call x0 -> x1, Pallas kernels: none -> 47.6 us  [on_device(): pl.pallas_call(functools.partial(kernel, tp, hh, entries, cache_len), out...]
    dot_general x9 -> x0, matrix products: 33.1 us -> none  [the longest x1 8.69 us: on_device(): jnp.einsum('tckb,ckbe->tce', picked, q_blocks, preferred_element_type=jnp...]
    unnamed x1 -> x0, blocking collectives: 26.2 us -> none
    unnamed x16 -> x0, local copies, waits for them, and re-layouts: 20 us -> none
    unnamed x2 -> x0, waiting for transfers between devices: 14.1 us -> none
    all_to_all x2 -> x0, local copies, waits for them, and re-layouts: 9.86 us -> none  [on_device(): lax.all_to_all(attended, 'tensor', split_axis=2, concat_axis=0, tiled=True)]
    all_gather x1 -> x0, blocking collectives: 8.84 us -> none  [on_device(): lax.all_gather(hidden_states, 'tensor', axis=0, tiled=True)]
    convert_element_type x7 -> x1, other arithmetic: 8.54 us -> 0.73 us  [on_device(): (lengths[:, None] + jnp.arange(NEW, dtype=jnp.int32)[None, :]).astype(F32)]
  transfers between devices with their start and end apart: 3 -> 0, of which waited for: 2 -> 0; matrix products, arithmetic and copies ran while one was open for 10% -> 0% of each run, Pallas kernels for 0% -> 0%
where the time goes in v1:
time: 59.3 us; the launch traced here: 58.8 us
  Pallas kernels  47.6 us (80%)
  local copies, waits for them, and re-layouts  8.12 us (14%)
  other arithmetic  2.44 us (4%)
  between operations  0.65 us (1%)
    pallas_call x1, Pallas kernels, on_device(): pl.pallas_call(functools.partial(kernel, tp, hh, entries, cache_len), out...  47.6 us
    reshape x1, local copies, waits for them, and re-layouts, on_device(): out.reshape(ROW_DEV, NEW, D)  1.67 us
    reshape x1, local copies, waits for them, and re-layouts, on_device(): hidden_states.reshape(OWN, D)  1.61 us
    reshape x1, local copies, waits for them, and re-layouts, on_device(): norm_gain.reshape(1, D)  1.34 us
    reshape x1, local copies, waits for them, and re-layouts, on_device(): q_rows.reshape(hh * KEEP)  1.34 us
    reshape x1, local copies, waits for them, and re-layouts, on_device(): new_kv.reshape(ROW_DEV, NEW, 2 * KVH * HD)  1.33 us

profile of v1, /device:TPU:0, one launch (start us, length us, event | category | flops | bytes accessed | tf_op | source)
XLA Modules:
  0.0 58.8 jit_solution(10483089287687869880)
XLA Ops:
  0.6 1.3 %reshape.59.q_rows = s32[512]{0:T(512)} reshape(s32[16,32]{1,0:T(8,128)} %param.14) | data formatting | bytes 4096 | tf_op jit(solution)/shard_map/reshape | solution.py:460
  2.0 0.7 %add_convert_fusion = f32[4,2]{1,0:T(4,128)S(1)} fusion(s32[4]{0:T(128)} %lengths.1), kind=kLoop, calls=%fused_computation.7 | loop fusion | flops 16 | bytes 48 | tf_op jit(solution)/shard_map/convert_element_type | solution.py:393
  2.7 0.1 convert_element_type.11
  2.8 0.9 %select_reduce_fusion = s32[64,16]{0,1:T(8,128)S(1)} fusion(s32[16,32]{1,0:T(8,128)S(1)} %multiply_add_fusion, s32[16,32]{1,0:T(8,128)} %param.18), kind=kLoop, calls=%fused_computation | loop fusion | flops 97280 | bytes 8192 | tf_op jit(solution)/shard_map/reduce_min | solution.py:400
  3.7 0.1 fusion
  3.8 0.7 %pad_maximum_fusion = (f32[8,128]{1,0:T(8,128)}, f32[8,128]{1,0:T(8,128)}) fusion(f32[8,64]{1,0:T(8,128)S(1)} %get-tuple-element.8, f32[8,64]{1,0:T(8,128)S(1)} %get-tuple-element.7, f32[8,64]{1,0:T(8,128)S(1)} %get-tuple-element.6), kind=kLoop, calls=%fused_computation.5 | loop fusion | flops 2048 | bytes 14336 | tf_op jit(solution)/shard_map/concatenate | solution.py:396
  4.5 0.1 copy.13
  4.6 0.7 %reshape.60.place = s32[1024]{0:T(1024)} reshape(s32[64,16]{1,0:T(8,128)S(1)} %copy.13) | data formatting | bytes 8192 | tf_op jit(solution)/shard_map/reshape | solution.py:400
  5.3 1.3 %reshape.58.gain = bf16[1,8192]{1,0:T(2,128)(2,1)} reshape(bf16[8192]{0:T(1024)(128)(2,1)} %param.12) | data formatting | bytes 32768 | tf_op jit(solution)/shard_map/reshape | solution.py:457
  6.6 1.6 %reshape.57.hidden = bf16[8,8192]{1,0:T(8,128)(2,1)} reshape(bf16[4,2,8192]{2,1,0:T(2,128)(2,1)} %param.11) | data formatting | bytes 262144 | tf_op jit(solution)/shard_map/reshape | solution.py:456
  8.2 47.6 %shard_map.122 = (bf16[8,8192]{1,0:T(8,128)(2,1)}, bf16[8,1024]{1,0:T(8,128)(2,1)}) custom-call(bf16[8,8192]{1,0:T(8,128)(2,1)} %reshape.57.hidden, bf16[1,8192]{1,0:T(2,128)(2,1)} %reshape.58.gain, f32[8,128]{1,0:T(8,128)} %get-tuple-element.9.cosine, f32[8,128]{1,0:T(8,128)} %get-tuple-element.10.sine, s32[512]{0:T(512)} %reshape.59.q_rows, s32[64]{0:T(128)} %kv_rows.1, ...), custom_call_target="tpu_custom_call" | custom-call | tf_op jit(solution)/shard_map/pallas_call | solution.py:410
  55.8 1.7 %reshape.61 = bf16[4,2,8192]{2,1,0:T(2,128)(2,1)} reshape(bf16[8,8192]{1,0:T(8,128)(2,1)} %get-tuple-element.4) | data formatting | bytes 262144 | tf_op jit(solution)/shard_map/reshape | solution.py:470
  57.5 1.3 %reshape.62 = bf16[4,2,1024]{2,1,0:T(2,128)(2,1)} reshape(bf16[8,1024]{1,0:T(8,128)(2,1)} %get-tuple-element.5) | data formatting | bytes 32768 | tf_op jit(solution)/shard_map/reshape | solution.py:470
  (2 shorter events, 0.0 us)

commit v2 on v1

--- a/solution.py
+++ b/solution.py
@@ -1,4 +1,5 @@
 import functools
+import math
 
 import jax
 import jax.numpy as jnp
@@ -33,11 +34,9 @@
     cache_len,
     hidden,
     gain,
-    cosine,
-    sine,
     q_rows,
     kv_rows,
-    place,
+    o_cols,
     lengths,
     q_hbm,
     kv_hbm,
@@ -66,6 +65,7 @@
     rbuf,
     sbuf,
     fbuf,
+    reached,
     q_sem,
     kv_sem,
     o_sem,
@@ -100,7 +100,7 @@
         for i in range(hh)
     ]
     kv_copy.start()
-    for copy in q_copies + k_copies + v_copies + o_copies:
+    for copy in q_copies:
         copy.start()
 
     def remote(src, dst, sems, slot, target):
@@ -119,17 +119,30 @@
             barrier, inc=1, device_id={"tensor": lax.rem(me + step, tp)}, device_id_type=MESH
         )
 
-    wide = hidden[...].astype(F32)
+    wide = jnp.concatenate([hidden[r].astype(F32) for r in range(ROW_DEV)], axis=0)
     inv_rms = lax.rsqrt(jnp.mean(wide * wide, axis=-1, keepdims=True) + 1e-05)
-    normed = (wide * inv_rms * gain[...].astype(F32)).astype(BF16).astype(F32)
+    normed = (wide * inv_rms * gain[...].astype(F32).reshape(1, D)).astype(BF16).astype(F32)
     for b in range(DB):
         nf[mc, b] = normed[:, b * BLK : (b + 1) * BLK]
     wo[hh * KEEP] = jnp.zeros((BLK, BLK), BF16)
 
+    lane = lax.broadcasted_iota(jnp.int32, (OWN, HD), 1)
+    row = lax.broadcasted_iota(jnp.int32, (OWN, HD), 0)
+    position = lax.rem(row, NEW)
+    for r in range(ROW_DEV):
+        position = position + jnp.where(row // NEW == r, lengths[r], 0)
+    exponent = lax.rem(lane, HD // 2).astype(F32) * (-math.log(500000.0) / (HD // 2))
+    angles = position.astype(F32) * jnp.exp(exponent)
+    cos_own = jnp.cos(angles)
+    sin_own = jnp.sin(angles)
+    sin_own = jnp.where(lane < HD // 2, -sin_own, sin_own)
+
     pl.semaphore_wait(barrier, tp - 1)
 
     x1 = remote(nf.at[mc], nf.at[mc], x1_sem, (0,), other)
     x1.start()
+    for copy in k_copies + v_copies:
+        copy.start()
     x1_in = remote(nf.at[1 - mc], nf.at[1 - mc], x1_sem, (0,), other)
     x1_in.wait_recv()
     xg[my] = jnp.concatenate([nf[0], nf[1]], axis=1).astype(BF16)
@@ -179,12 +192,14 @@
 
     for copy in q_copies:
         copy.wait()
+    for copy in o_copies:
+        copy.start()
 
     def query_pair(pair, carry):
         parts = []
         for s in range(2):
             c = pair * 2 + s
-            x = picked([q_rows[c * KEEP + k] for k in range(KEEP)])
+            x = picked([q_rows[c, k] for k in range(KEEP)])
             w = wq[c].reshape(KEEP * BLK, BLK)
             parts.append(jnp.dot(x, w, preferred_element_type=F32))
         for d in range(tp):
@@ -201,8 +216,6 @@
         sends.append(copy)
     qr[me] = qs[me]
 
-    cos_own = cosine[...]
-    sin_own = sine[...]
     for step in range(1, tp):
         source = lax.rem(me + tp - step, tp)
         remote(ks.at[source], kr.at[source], ka_sem, (step,), source).wait_recv()
@@ -219,7 +232,8 @@
             total = total * cos_own + pltpu.roll(total, HD // 2, 1) * sin_own
         fresh.append(total)
     fresh = jnp.concatenate(fresh, axis=1).astype(BF16)
-    new_kv[...] = fresh
+    for r in range(ROW_DEV):
+        new_kv[r] = fresh.astype(F32)[r * NEW : (r + 1) * NEW].astype(BF16)
     tail = jnp.concatenate(
         [fresh.astype(F32), jnp.zeros((PAD - OWN, 2 * KVH * HD), F32)], axis=0
     ).astype(BF16)
@@ -311,12 +325,20 @@
         def one_pair(pair, inner):
             n = (ch * pairs + pair) * 2
             total = None
+            ahead = [reached[i] for i in range(hh)]
+            slots = []
+            for a in range(2):
+                for i in range(hh):
+                    at = ahead[i]
+                    hit = o_cols[i, jnp.minimum(at, KEEP - 1)] == n + a
+                    slots.append(jnp.where(hit, i * KEEP + at, hh * KEEP))
+                    ahead[i] = at + hit.astype(jnp.int32)
             wide_k = 2 if hh % 2 == 0 else 1
             for i in range(0, hh, wide_k):
                 w = jnp.concatenate(
                     [
                         jnp.concatenate(
-                            [wo[place[(n + a) * hh + i + b]] for b in range(wide_k)], axis=0
+                            [wo[slots[a * hh + i + b]] for b in range(wide_k)], axis=0
                         )
                         for a in range(2)
                     ],
@@ -329,6 +351,8 @@
             columns = pl.ds(pl.multiple_of(pair * 2 * BLK, 2 * BLK), 2 * BLK)
             for c in range(2):
                 pbuf[ch, c, :, columns] = total[c * side : (c + 1) * side]
+            for i in range(hh):
+                reached[i] = ahead[i]
             return inner
 
         lax.fori_loop(0, pairs, one_pair, 0)
@@ -340,6 +364,8 @@
 
         return carry
 
+    for i in range(hh):
+        reached[i] = 0
     lax.fori_loop(0, CHUNKS, project, 0)
     pass_on(CHUNKS - 1)
 
@@ -352,7 +378,9 @@
             ).wait_recv()
             total = total + fbuf[ch, source]
         wide_chunk = D // CHUNKS
-        out[:, pl.ds(pl.multiple_of(ch * wide_chunk, wide_chunk), wide_chunk)] = total.astype(BF16)
+        columns = pl.ds(pl.multiple_of(ch * wide_chunk, wide_chunk), wide_chunk)
+        for r in range(ROW_DEV):
+            out[r, :, columns] = total[r * NEW : (r + 1) * NEW].astype(BF16)
         return carry
 
     lax.fori_loop(0, CHUNKS, finish, 0)
@@ -388,17 +416,6 @@
     entries = kv_blocks.shape[0]
     cache_len = key_cache.shape[1]
     ny = tp // 2
-    half = HD // 2
-    frequency = 500000.0 ** (-jnp.arange(half, dtype=F32) / half)
-    positions = (lengths[:, None] + jnp.arange(NEW, dtype=jnp.int32)[None, :]).astype(F32)
-    angles = positions.reshape(OWN, 1) * frequency
-    cos_half, sin_half = jnp.cos(angles), jnp.sin(angles)
-    cosine = jnp.concatenate([cos_half, cos_half], axis=-1)
-    sine = jnp.concatenate([-sin_half, sin_half], axis=-1)
-    slot = jnp.arange(hh * KEEP, dtype=jnp.int32).reshape(hh, KEEP)
-    hit = o_cols[None] == jnp.arange(DB, dtype=jnp.int32)[:, None, None]
-    place = jnp.min(jnp.where(hit, slot[None], hh * KEEP), axis=-1).reshape(DB * hh)
-
     vmem = pl.BlockSpec(memory_space=pltpu.VMEM)
     smem = pl.BlockSpec(memory_space=pltpu.SMEM)
     anywhere = pl.BlockSpec(memory_space=pl.ANY)
@@ -407,13 +424,13 @@
     width = cache_len + PAD
     chunk = D // CHUNKS
     dma = pltpu.SemaphoreType.DMA
-    out, new_kv = pl.pallas_call(
+    return pl.pallas_call(
         functools.partial(kernel, tp, hh, entries, cache_len),
         out_shape=(
-            jax.ShapeDtypeStruct((OWN, D), BF16),
-            jax.ShapeDtypeStruct((OWN, 2 * KVH * HD), BF16),
+            jax.ShapeDtypeStruct((ROW_DEV, NEW, D), BF16),
+            jax.ShapeDtypeStruct((ROW_DEV, NEW, 2 * KVH * HD), BF16),
         ),
-        in_specs=[vmem] * 4 + [smem] * 4 + [anywhere] * 5,
+        in_specs=[vmem] * 2 + [smem] * 4 + [anywhere] * 5,
         out_specs=(vmem, vmem),
         scratch_shapes=[
             pltpu.VMEM((hh, KEEP, BLK, BLK), BF16),
@@ -436,6 +453,7 @@
             pltpu.VMEM((CHUNKS, ny * OWN, chunk), F32),
             pltpu.VMEM((CHUNKS, ny * OWN, chunk), F32),
             pltpu.VMEM((CHUNKS, ny, OWN, chunk), F32),
+            pltpu.SMEM((hh,), jnp.int32),
             dma((hh,)),
             dma,
             dma((hh,)),
@@ -453,13 +471,11 @@
             collective_id=0, has_side_effects=True, vmem_limit_bytes=60 * 1024 * 1024
         ),
     )(
-        hidden_states.reshape(OWN, D),
-        norm_gain.reshape(1, D),
-        cosine,
-        sine,
-        q_rows.reshape(hh * KEEP),
+        hidden_states,
+        norm_gain,
+        q_rows,
         kv_rows,
-        place,
+        o_cols,
         lengths,
         q_blocks,
         kv_blocks,
@@ -467,7 +483,6 @@
         key_cache,
         value_cache,
     )
-    return out.reshape(ROW_DEV, NEW, D), new_kv.reshape(ROW_DEV, NEW, 2 * KVH * HD)
 
 
 def solution(mesh):

time: 59.3 us -> 48.5 us (0.82)
  local copies, waits for them, and re-layouts: 8.12 us -> 2.98 us
  Pallas kernels: 47.6 us -> 44.6 us
  other arithmetic: 2.44 us -> 0 us
    reshape x6 -> x0, local copies, waits for them, and re-layouts: 7.96 us -> none  [the longest x1 1.67 us: on_device(): out.reshape(ROW_DEV, NEW, D)]
    unnamed x0 -> x2, local copies, waits for them, and re-layouts: none -> 2.98 us
    pallas_call x1, Pallas kernels: 47.6 us -> 44.6 us  [on_device(): pl.pallas_call(functools.partial(kernel, tp, hh, entries, cache_len), out...]
    reduce_min x1 -> x0, other arithmetic: 0.92 us -> none  [on_device(): jnp.min(jnp.where(hit, slot[None], hh * KEEP), axis=-1).reshape(DB * hh)]
    convert_element_type x1 -> x0, other arithmetic: 0.73 us -> none  [on_device(): (lengths[:, None] + jnp.arange(NEW, dtype=jnp.int32)[None, :]).astype(F32)]
    concatenate x1 -> x0, other arithmetic: 0.67 us -> none  [on_device(): cosine = jnp.concatenate([cos_half, cos_half], axis=-1)]
where the time goes in v2:
time: 48.5 us; the launch traced here: 48.3 us
  Pallas kernels  44.6 us (92%)
  local copies, waits for them, and re-layouts  2.98 us (6%)
  between operations  0.64 us (1%)
    pallas_call x1, Pallas kernels, on_device(): pl.pallas_call(functools.partial(kernel, tp, hh, entries, cache_len), out...  44.6 us
    unnamed x2, local copies, waits for them, and re-layouts  2.98 us

profile of v2, /device:TPU:0, one launch (start us, length us, event | category | flops | bytes accessed | tf_op | source)
XLA Modules:
  0.0 48.3 jit_solution(10905858228228156916)
XLA Ops:
  0.6 44.6 %shard_map.122 = (bf16[4,2,8192]{2,1,0:T(2,128)(2,1)}, bf16[4,2,1024]{2,1,0:T(2,128)(2,1)}) custom-call(bf16[4,2,8192]{2,1,0:T(2,128)(2,1)} %hidden.1, bf16[8192]{0:T(1024)(128)(2,1)} %gain.1, s32[16,32]{1,0:T(8,128)} %q_rows.1, s32[64]{0:T(128)} %kv_rows.1, s32[16,32]{1,0:T(8,128)} %o_cols.1, s32[4]{0:T(128)} %lengths.1, bf16[16,32,128,128]{3,2,1,0:T(8,128)(2,1)} %q_hbm.1, ...), custom_call_target="tpu_custom_call" | custom-call | tf_op jit(solution)/shard_map/pallas_call | solution.py:427
  45.3 1.7 %copy.15 = bf16[4,2,8192]{2,1,0:T(2,128)(2,1)} copy(bf16[4,2,8192]{2,1,0:T(2,128)(2,1)} %get-tuple-element.4) | data formatting | bytes 262144
  46.9 1.3 %copy.16 = bf16[4,2,1024]{2,1,0:T(2,128)(2,1)} copy(bf16[4,2,1024]{2,1,0:T(2,128)(2,1)} %get-tuple-element.5) | data formatting | bytes 32768

commit v3 on v2

--- a/solution.py
+++ b/solution.py
@@ -22,6 +22,10 @@
 GROUP = QH // KVH
 PAD = 128
 CHUNKS = 8
+PIECES = 2
+UO = 4
+UA = 4
+UQ = 4
 MESH = pl.DeviceIdType.MESH
 F32 = jnp.float32
 BF16 = jnp.bfloat16
@@ -32,12 +36,12 @@
     hh,
     entries,
     cache_len,
-    hidden,
-    gain,
-    q_rows,
-    kv_rows,
-    o_cols,
     lengths,
+    hidden_hbm,
+    gain_hbm,
+    q_rows_hbm,
+    kv_rows_hbm,
+    o_cols_hbm,
     q_hbm,
     kv_hbm,
     o_hbm,
@@ -50,7 +54,7 @@
     wo,
     kbuf,
     vbuf,
-    nf,
+    xs,
     xg,
     qs,
     qr,
@@ -66,6 +70,12 @@
     sbuf,
     fbuf,
     reached,
+    hidden,
+    gain,
+    q_rows,
+    kv_rows,
+    o_cols,
+    in_sem,
     q_sem,
     kv_sem,
     o_sem,
@@ -85,6 +95,22 @@
     mc = lax.rem(me, 2)
     other = my * 2 + (1 - mc)
 
+    barrier = pltpu.get_barrier_semaphore()
+    for step in range(1, tp):
+        pl.semaphore_signal(
+            barrier, inc=1, device_id={"tensor": lax.rem(me + step, tp)}, device_id_type=MESH
+        )
+
+    fetched = (
+        (hidden_hbm, hidden),
+        (gain_hbm, gain),
+        (q_rows_hbm, q_rows),
+        (kv_rows_hbm, kv_rows),
+        (o_cols_hbm, o_cols),
+    )
+    in_copies = [pltpu.make_async_copy(a, b, in_sem.at[i]) for i, (a, b) in enumerate(fetched)]
+    for copy in in_copies:
+        copy.start()
     q_copies = [pltpu.make_async_copy(q_hbm.at[c], wq.at[c], q_sem.at[c]) for c in range(hh)]
     kv_copy = pltpu.make_async_copy(kv_hbm, wkv, kv_sem)
     k_copies = [
@@ -113,17 +139,14 @@
             device_id_type=MESH,
         )
 
-    barrier = pltpu.get_barrier_semaphore()
-    for step in range(1, tp):
-        pl.semaphore_signal(
-            barrier, inc=1, device_id={"tensor": lax.rem(me + step, tp)}, device_id_type=MESH
-        )
-
+    for copy in in_copies:
+        copy.wait()
     wide = jnp.concatenate([hidden[r].astype(F32) for r in range(ROW_DEV)], axis=0)
     inv_rms = lax.rsqrt(jnp.mean(wide * wide, axis=-1, keepdims=True) + 1e-05)
     normed = (wide * inv_rms * gain[...].astype(F32).reshape(1, D)).astype(BF16).astype(F32)
-    for b in range(DB):
-        nf[mc, b] = normed[:, b * BLK : (b + 1) * BLK]
+    for b in range(0, DB, 2):
+        both = [normed[:, n * BLK : (n + 1) * BLK] for n in (b, b + 1)]
+        xs[me, b * OWN : (b + 2) * OWN] = jnp.concatenate(both, axis=0).astype(BF16)
     wo[hh * KEEP] = jnp.zeros((BLK, BLK), BF16)
 
     lane = lax.broadcasted_iota(jnp.int32, (OWN, HD), 1)
@@ -139,35 +162,43 @@
 
     pl.semaphore_wait(barrier, tp - 1)
 
-    x1 = remote(nf.at[mc], nf.at[mc], x1_sem, (0,), other)
+    piece_rows = DB * OWN // PIECES
+    pieces = [pl.ds(p * piece_rows, piece_rows) for p in range(PIECES)]
+    x2 = []
+    for p in range(PIECES):
+        for step in range(1, ny):
+            to = lax.rem(my + step, ny)
+            part = xs.at[me, pieces[p]]
+            copy = remote(part, part, x2_sem, (step, p), to * 2 + mc)
+            copy.start()
+            x2.append(copy)
+    x1 = remote(xs.at[me], xs.at[me], x1_sem, (0,), other)
     x1.start()
     for copy in k_copies + v_copies:
         copy.start()
-    x1_in = remote(nf.at[1 - mc], nf.at[1 - mc], x1_sem, (0,), other)
-    x1_in.wait_recv()
-    xg[my] = jnp.concatenate([nf[0], nf[1]], axis=1).astype(BF16)
-
-    half = DB // 2
-    mine = pl.ds(mc * half, half)
-    theirs = pl.ds((1 - mc) * half, half)
-    x2 = []
-    for step in range(1, ny):
-        to = lax.rem(my + step, ny)
-        copy = remote(xg.at[my, mine], xg.at[my, mine], x2_sem, (step,), to * 2 + mc)
-        copy.start()
-        x2.append(copy)
+
+    def assemble(y):
+        sides = [xs[y * 2 + c].astype(F32).reshape(DB, OWN, BLK) for c in range(2)]
+        xg[y] = jnp.concatenate(sides, axis=1).astype(BF16)
+
+    remote(xs.at[other], xs.at[other], x1_sem, (0,), other).wait_recv()
+    assemble(my)
+
     x3 = []
+    for p in range(PIECES):
+        for step in range(1, ny):
+            source = lax.rem(my + ny - step, ny)
+            part = xs.at[source * 2 + mc, pieces[p]]
+            remote(part, part, x2_sem, (step, p), other).wait_recv()
+            copy = remote(part, part, x3_sem, (step, p), other)
+            copy.start()
+            x3.append(copy)
     for step in range(1, ny):
         source = lax.rem(my + ny - step, ny)
-        piece = xg.at[source, mine]
-        remote(piece, piece, x2_sem, (step,), other).wait_recv()
-        copy = remote(piece, piece, x3_sem, (step,), other)
-        copy.start()
-        x3.append(copy)
-    for step in range(1, ny):
-        source = lax.rem(my + ny - step, ny)
-        piece = xg.at[source, theirs]
-        remote(piece, piece, x3_sem, (step,), other).wait_recv()
+        for p in range(PIECES):
+            part = xs.at[source * 2 + 1 - mc, pieces[p]]
+            remote(part, part, x3_sem, (step, p), other).wait_recv()
+        assemble(source)
 
     def picked(rows):
         blocks = [jnp.concatenate([xg[y, row] for y in range(ny)], axis=0) for row in rows]
@@ -207,7 +238,7 @@
             qs[d, pl.ds(pl.multiple_of(pair * 16, 16), 16)] = both.astype(BF16)
         return carry
 
-    lax.fori_loop(0, hh // 2, query_pair, 0)
+    lax.fori_loop(0, hh // 2, query_pair, 0, unroll=UQ)
     slab = hh * OWN
     for step in range(1, tp):
         to = lax.rem(me + step, tp)
@@ -282,7 +313,7 @@
                 ]
         return carry
 
-    lax.fori_loop(0, ROW_DEV, attend_row, 0)
+    lax.fori_loop(0, ROW_DEV, attend_row, 0, unroll=UA)
 
     for d in range(tp):
         asend[d] = af[pl.ds(d * slab, slab)].astype(BF16)
@@ -355,7 +386,7 @@
                 reached[i] = ahead[i]
             return inner
 
-        lax.fori_loop(0, pairs, one_pair, 0)
+        lax.fori_loop(0, pairs, one_pair, 0, unroll=UO)
         stage1(ch).start()
 
         @pl.when(ch > 0)
@@ -418,7 +449,7 @@
     ny = tp // 2
     vmem = pl.BlockSpec(memory_space=pltpu.VMEM)
     smem = pl.BlockSpec(memory_space=pltpu.SMEM)
-    anywhere = pl.BlockSpec(memory_space=pl.ANY)
+    hbm = pl.BlockSpec(memory_space=pltpu.HBM)
     slab = hh * OWN
     cols = max(1, entries // KEEP)
     width = cache_len + PAD
@@ -430,7 +461,7 @@
             jax.ShapeDtypeStruct((ROW_DEV, NEW, D), BF16),
             jax.ShapeDtypeStruct((ROW_DEV, NEW, 2 * KVH * HD), BF16),
         ),
-        in_specs=[vmem] * 2 + [smem] * 4 + [anywhere] * 5,
+        in_specs=[smem] + [hbm] * 10,
         out_specs=(vmem, vmem),
         scratch_shapes=[
             pltpu.VMEM((hh, KEEP, BLK, BLK), BF16),
@@ -438,7 +469,7 @@
             pltpu.VMEM((hh * KEEP + 1, BLK, BLK), BF16),
             pltpu.VMEM((ROW_DEV, width, KVH * HD), BF16),
             pltpu.VMEM((ROW_DEV, width, KVH * HD), BF16),
-            pltpu.VMEM((2, DB, OWN, BLK), F32),
+            pltpu.VMEM((tp, DB * OWN, BLK), BF16),
             pltpu.VMEM((ny, DB, 2 * OWN, BLK), BF16),
             pltpu.VMEM((tp, slab, HD), BF16),
             pltpu.VMEM((tp, slab, HD), BF16),
@@ -454,13 +485,19 @@
             pltpu.VMEM((CHUNKS, ny * OWN, chunk), F32),
             pltpu.VMEM((CHUNKS, ny, OWN, chunk), F32),
             pltpu.SMEM((hh,), jnp.int32),
+            pltpu.VMEM((ROW_DEV, NEW, D), BF16),
+            pltpu.VMEM((D,), BF16),
+            pltpu.SMEM((hh, KEEP), jnp.int32),
+            pltpu.SMEM((entries,), jnp.int32),
+            pltpu.SMEM((hh, KEEP), jnp.int32),
+            dma((5,)),
             dma((hh,)),
             dma,
             dma((hh,)),
             dma((2, ROW_DEV)),
             dma((2, 1)),
-            dma((2, ny)),
-            dma((2, ny)),
+            dma((2, ny, PIECES)),
+            dma((2, ny, PIECES)),
             dma((2, tp)),
             dma((2, tp)),
             dma((2, tp)),
@@ -471,12 +508,12 @@
             collective_id=0, has_side_effects=True, vmem_limit_bytes=60 * 1024 * 1024
         ),
     )(
+        lengths,
         hidden_states,
         norm_gain,
         q_rows,
         kv_rows,
         o_cols,
-        lengths,
         q_blocks,
         kv_blocks,
         o_blocks,

time: 48.5 us -> 44.2 us (0.911)
  Pallas kernels: 44.6 us -> 40.4 us
    pallas_call x1, Pallas kernels: 44.6 us -> 40.4 us  [on_device(): pl.pallas_call(functools.partial(kernel, tp, hh, entries, cache_len), out...]
where the time goes in v3:
time: 44.2 us; the launch traced here: 44 us
  Pallas kernels  40.4 us (91%)
  local copies, waits for them, and re-layouts  2.98 us (7%)
  between operations  0.64 us (1%)
    pallas_call x1, Pallas kernels, on_device(): pl.pallas_call(functools.partial(kernel, tp, hh, entries, cache_len), out...  40.4 us
    unnamed x2, local copies, waits for them, and re-layouts  2.98 us

profile of v3, /device:TPU:0, one launch (start us, length us, event | category | flops | bytes accessed | tf_op | source)
XLA Modules:
  0.0 44.0 jit_solution(7239413800372427474)
XLA Ops:
  0.6 40.4 %shard_map.122 = (bf16[4,2,8192]{2,1,0:T(2,128)(2,1)}, bf16[4,2,1024]{2,1,0:T(2,128)(2,1)}) custom-call(s32[4]{0:T(128)} %lengths.1, bf16[4,2,8192]{2,1,0:T(2,128)(2,1)} %hidden_hbm.1, bf16[8192]{0:T(1024)(128)(2,1)} %gain_hbm.1, s32[16,32]{1,0:T(8,128)} %q_rows_hbm.1, s32[64]{0:T(128)} %kv_rows_hbm.1, s32[16,32]{1,0:T(8,128)} %o_cols_hbm.1, ...), custom_call_target="tpu_custom_call" | custom-call | tf_op jit(solution)/shard_map/pallas_call | solution.py:458
  41.0 1.7 %copy.15 = bf16[4,2,8192]{2,1,0:T(2,128)(2,1)} copy(bf16[4,2,8192]{2,1,0:T(2,128)(2,1)} %get-tuple-element.4) | data formatting | bytes 262144
  42.7 1.3 %copy.16 = bf16[4,2,1024]{2,1,0:T(2,128)(2,1)} copy(bf16[4,2,1024]{2,1,0:T(2,128)(2,1)} %get-tuple-element.5) | data formatting | bytes 32768

commit v4 on v3

--- a/solution.py
+++ b/solution.py
@@ -429,6 +429,11 @@
     lax.fori_loop(0, CHUNKS, drain, 0)
 
 
+def hand_over(attn, fresh, attn_out, fresh_out):
+    attn_out[...] = attn[...]
+    fresh_out[...] = fresh[...]
+
+
 def on_device(
     tp,
     hidden_states,
@@ -455,7 +460,7 @@
     width = cache_len + PAD
     chunk = D // CHUNKS
     dma = pltpu.SemaphoreType.DMA
-    return pl.pallas_call(
+    results = pl.pallas_call(
         functools.partial(kernel, tp, hh, entries, cache_len),
         out_shape=(
             jax.ShapeDtypeStruct((ROW_DEV, NEW, D), BF16),
@@ -520,6 +525,12 @@
         key_cache,
         value_cache,
     )
+    return pl.pallas_call(
+        hand_over,
+        out_shape=tuple(jax.ShapeDtypeStruct(r.shape, r.dtype) for r in results),
+        in_specs=[vmem] * 2,
+        out_specs=(vmem, vmem),
+    )(*results)
 
 
 def solution(mesh):

time: 44.2 us -> 42.7 us (0.966)
  local copies, waits for them, and re-layouts: 2.98 us -> 0 us
  Pallas kernels: 40.4 us -> 41.9 us
    unnamed x2 -> x0, local copies, waits for them, and re-layouts: 2.98 us -> none
    pallas_call x0 -> x1, Pallas kernels: none -> 1.57 us  [on_device(): pl.pallas_call(hand_over, out_shape=tuple((jax.ShapeDtypeStruct(r.shape,...]
where the time goes in v4:
time: 42.7 us; the launch traced here: 42.6 us
  Pallas kernels  41.9 us (98%)
  between operations  0.64 us (1%)
    pallas_call x1, Pallas kernels, on_device(): pl.pallas_call(functools.partial(kernel, tp, hh, entries, cache_len), out...  40.4 us
    pallas_call x1, Pallas kernels, on_device(): pl.pallas_call(hand_over, out_shape=tuple((jax.ShapeDtypeStruct(r.shape,...  1.57 us

profile of v4, /device:TPU:0, one launch (start us, length us, event | category | flops | bytes accessed | tf_op | source)
XLA Modules:
  0.0 42.6 jit_solution(6670799728147141201)
XLA Ops:
  0.6 40.4 %shard_map.122 = (bf16[4,2,8192]{2,1,0:T(2,128)(2,1)}, bf16[4,2,1024]{2,1,0:T(2,128)(2,1)}) custom-call(s32[4]{0:T(128)} %lengths.1, bf16[4,2,8192]{2,1,0:T(2,128)(2,1)} %hidden_hbm.1, bf16[8192]{0:T(1024)(128)(2,1)} %gain_hbm.1, s32[16,32]{1,0:T(8,128)} %q_rows_hbm.1, s32[64]{0:T(128)} %kv_rows_hbm.1, s32[16,32]{1,0:T(8,128)} %o_cols_hbm.1, ...), custom_call_target="tpu_custom_call" | custom-call | tf_op jit(solution)/shard_map/pallas_call | solution.py:463
  41.0 1.6 %shard_map.123 = (bf16[4,2,8192]{2,1,0:T(2,128)(2,1)}, bf16[4,2,1024]{2,1,0:T(2,128)(2,1)}) custom-call(bf16[4,2,8192]{2,1,0:T(2,128)(2,1)} %get-tuple-element.4.attn, bf16[4,2,1024]{2,1,0:T(2,128)(2,1)} %get-tuple-element.5.fresh), custom_call_target="tpu_custom_call" | custom-call | tf_op jit(solution)/shard_map/pallas_call | solution.py:528
